TPU v7x, 256 devices: a whole 4x4x8 slice. The times are simulated.
256 devices in a mesh: aux: 64 (over y, z, core), occ: 4 (over x).
Axes of the slice: x: 4, y: 4, z: 8, core: 2. Of those that a mesh axis runs over, the one named last changes fastest.
Arguments:
- integrals: bfloat16 [8192, 64, 512], P('aux'), may hold values from -6 to 6
- slot_row_block: int32 [8192], P('aux'), may hold values from 0 to 511
- slot_column_block: int32 [8192], P('aux'), may hold values from 0 to 511
- shard_live_slots: int32 [64], P('aux'), may hold values from 32 to 128, as said below
- orbitals: bfloat16 [128, 32768], P('occ'), may hold values from -0.06982422 to 0.06982422
Outputs:
- exchange_applied: float32 [128, 32768], P(None, ('aux', 'occ'))
Inputs may be any that keep to these rules, and one draw needn't show every extreme that they name: `shard_live_slots`: some shard has all 128 slots live in every draw.
All inputs are finite; a program needn't handle non-finite values.
Results may differ from a plain program's by a relative error of at most 0.0033.
Values may be sent and summed in bfloat16 or wider, within the bound.
A program may use at most 256 MiB of HBM per device.

v0:
```python
import jax
import jax.numpy as jnp
from jax import lax
from jax.sharding import PartitionSpec as P


def shards(integrals, slot_row_block, slot_column_block, shard_live_slots, orbitals):
    occ_group, basis_len = orbitals.shape
    slot_count, block_len, packed = integrals.shape
    block_total = basis_len // block_len
    aux_here = packed // block_len
    orb_blocks = orbitals.reshape(occ_group, block_total, block_len)
    picked = jnp.take(orb_blocks, slot_column_block, axis=1)
    contrib = jnp.einsum("jkl,klx->kjx", picked, integrals, preferred_element_type=jnp.float32)
    live_slot = jnp.arange(slot_count, dtype=jnp.int32) < shard_live_slots[0]
    contrib = jnp.where(live_slot[:, None, None], contrib, jnp.float32(0.0))
    half_done = (
        jnp.zeros((block_total, occ_group, packed), jnp.float32).at[slot_row_block].add(contrib)
    )
    half_done = half_done.astype(jnp.bfloat16)
    split_half = half_done.reshape(block_total, occ_group, aux_here, block_len)
    segment = lax.all_gather(orbitals, "occ", axis=0, tiled=True)
    orb_part = segment.reshape(segment.shape[0], block_total, block_len)
    fitted = jnp.einsum(
        "rjpx,irx->pji", split_half, orb_part, preferred_element_type=jnp.float32
    ).astype(jnp.bfloat16)
    partial_value = jnp.einsum(
        "pji,rjpx->irx", fitted, split_half, preferred_element_type=jnp.float32
    )
    partial_value = partial_value.reshape(partial_value.shape[0], basis_len)
    return lax.psum_scatter(partial_value, ("aux", "occ"), scatter_dimension=1, tiled=True)


def solution(mesh):
    placed = (P("aux", None, None), P("aux"), P("aux"), P("aux"), P("occ", None))
    return jax.shard_map(
        shards, mesh=mesh, in_specs=placed, out_specs=P(None, ("aux", "occ")), check_vma=False
    )
```

profile of v0, /device:TPU:6, one launch (start us, length us, event | category | flops | bytes accessed | tf_op | source)
XLA Modules:
  0.0 1556.3 jit_solution(10911459779983764951)
XLA Ops:
  6.5 0.0 copy-start
  6.5 0.0 all-gather.2.cloned.1.call-start
  6.5 0.7 all-gather.2.cloned.1.call-update
  7.3 0.0 copy-start.1
  7.3 0.0 reduce-scatter.2.cloned.1.call-start
  7.3 6.5 reshape.20
  14.4 6.9 copy.17
  21.3 0.0 copy-done
  21.3 3.0 gather_fusion
  24.4 0.0 copy-done.1
  24.4 8.9 broadcast_select_fusion
  33.3 11.4 broadcast_in_dim.31
  44.7 26.9 %scatter_fusion = f32[512,32,512]{2,1,0:T(8,128)} fusion(f32[512,32,512]{2,1,0:T(8,128)} %broadcast_in_dim.31, s32[128]{0:T(128)S(1)} %compare_select_fusion.1, f32[128,32,512]{2,1,0:T(8,128)} %broadcast_select_fusion), kind=kCustom, calls=%fused_computation.1 | custom fusion | flops 2097152 | bytes 25166336 | tf_op jit(solution)/shard_map/scatter-add | solution.py:18
  71.5 17.6 %convert_element_type.9 = bf16[512,32,512]{2,1,0:T(8,128)(2,1)} convert(f32[512,32,512]{2,1,0:T(8,128)} %scatter_fusion) | non-fusion elementwise | flops 8388608 | bytes 50331648 | tf_op jit(solution)/shard_map/convert_element_type | solution.py:20
  89.1 26.3 %copy.18 = bf16[512,32,512]{0,2,1:T(8,128)(2,1)} copy(bf16[512,32,512]{2,1,0:T(8,128)(2,1)} %convert_element_type.9) | data formatting | bytes 33554432 | tf_op jit(solution)/shard_map/convert_element_type | solution.py:20
  115.4 30.0 %copy.21 = bf16[512,64,32,8]{1,0,3,2:T(8,128)(2,1)} copy(bf16[512,64,32,8]{0,1,3,2:T(8,128)(2,1)} %bitcast.65) | data formatting | bytes 33554432 | tf_op jit(solution)/shard_map/pji,rjpx->irx/dot_general | solution.py:27
  145.4 38.3 %dot_general.16 = bf16[32768,32,8]{0,2,1:T(8,128)(2,1)} reshape(bf16[512,64,32,8]{1,0,3,2:T(8,128)(2,1)} %copy.21) | data formatting | bytes 33554432 | tf_op jit(solution)/shard_map/pji,rjpx->irx/dot_general | solution.py:27
  183.7 36.2 %copy.20 = bf16[512,32,8,64]{3,2,0,1:T(8,128)(2,1)} copy(bf16[512,32,8,64]{0,3,2,1:T(8,128)(2,1)} %bitcast.66) | data formatting | bytes 33554432 | tf_op jit(solution)/shard_map/reshape | solution.py:21
  219.9 0.0 all-gather.2.cloned.1.call-done
  219.9 11.9 copy.19
  231.9 16.0 %fusion.29 = bf16[8,32,128]{2,0,1:T(8,128)(2,1)S(1)} fusion(bf16[128,512,64,1]{0,2,1,3:T(8,128)(2,1)} %bitcast.67, bf16[512,32,8,64]{3,2,0,1:T(8,128)(2,1)} %copy.20), kind=kOutput, calls=%bitcast_fusion.clone.1 | convolution fusion | flops 2147516416 | bytes 25231360 | tf_op jit(solution)/shard_map/rjpx,irx->pji/dot_general | solution.py:24
  247.9 10.5 convolution_bitcast_fusion
  258.4 0.0 reduce-scatter.2.cloned.1.call-update
  258.4 1291.1 %reduce-scatter.2.cloned.1.call-done = f32[128,128]{1,0:T(8,128)} async-done(((f32[128,32768]{1,0:T(8,128)}), f32[128,128]{1,0:T(8,128)}) %reduce-scatter.2.cloned.1.call-update) | async-done | bytes 65552 | tf_op jit(solution)/shard_map/reduce_scatter | solution.py:31
  (4 shorter events, 0.0 us)
Async XLA Ops:
  6.5 14.8 copy-start
  6.5 213.4 %all-gather.2.cloned.1.call-start = ((), (), s32[]{:S(2)}) async-start(), calls=%async_computation.1 | async-start | bytes 10485760 | tf_op jit(solution)/shard_map/all_gather | solution.py:22
  7.3 17.1 %copy-start.1 = (s32[128]{0:T(128)S(1)}, s32[128]{0:T(128)}, u32[]{:S(2)}) copy-start(s32[128]{0:T(128)} %param.6) | copy-start | bytes 1540
  7.3 1542.2 %reduce-scatter.2.cloned.1.call-start = ((), (), s32[]{:S(2)}) async-start(), calls=%async_computation.2 | async-start | bytes 16842752 | tf_op jit(solution)/shard_map/reduce_scatter | solution.py:31
Sparse Core Ops, SparseCore 0:
  9.2 87.3 all-gather.1
  258.5 1290.9 reduce-scatter.1
where the time goes:
time: 1570 us; the launch traced here: 1560 us
  waiting for transfers between devices  1290 us (82%)
  local copies, waits for them, and re-layouts  170 us (11%)
  other arithmetic  44.5 us (3%)
  matrix products  35.4 us (2%)
    reduce_scatter x1, waiting for transfers between devices, shards(): lax.psum_scatter(partial_value, ('aux', 'occ'), scatter_dimension=1, tile...  1290 us
    dot_general x2, local copies, waits for them, and re-layouts, shards(): jnp.einsum('pji,rjpx->irx', fitted, split_half, preferred_element_type=jn...  68.3 us
    reshape x1, local copies, waits for them, and re-layouts, shards(): split_half = half_done.reshape(block_total, occ_group, aux_here, block_len)  36.2 us
  transfers between devices with their start and end apart: 2, of which 1 were waited for; matrix products, arithmetic and copies ran while one was open for 14% of the time, Pallas kernels for 0%

commit v1 on v0

v1 whole, which is shorter than its diff:
```python
import functools

import jax
import jax.numpy as jnp
from jax import lax
from jax.experimental import pallas as pl
from jax.experimental.pallas import tpu as pltpu
from jax.sharding import PartitionSpec as P

MESH = pl.DeviceIdType.MESH
SLOTS = 128
SIDE = 64
NAUX = 8
NCHUNK = 8
CSLOTS = SLOTS // NCHUNK
CL = CSLOTS * SIDE
F32 = jnp.float32
BF16 = jnp.bfloat16


def swap_halves(v):
    return pltpu.roll(v, SIDE, v.ndim - 1)


def low_lanes(shape):
    return lax.broadcasted_iota(jnp.int32, shape, len(shape) - 1) < SIDE


def gather_pair(table, i0, i1):
    a, b = table[i0], table[i1]
    return jnp.where(low_lanes(a.shape), a, b)


def exchange_kernel(cols, rows, integrals, orbitals, out,
                    orb, table, ints, gath, rbuf, hbuf, facc,
                    orb_sem, int_sem, send_l, send_r, send_f, recv_l, recv_r, recv_f):
    aux, me = lax.axis_index("aux"), lax.axis_index("occ")
    right, left = lax.rem(me + 1, 4), lax.rem(me + 3, 4)
    orb_copy = pltpu.make_async_copy(orbitals, orb, orb_sem)
    orb_copy.start()

    def int_copy(c):
        return pltpu.make_async_copy(
            integrals.at[pl.ds(c * CSLOTS, CSLOTS)], ints.at[pl.ds(c * CSLOTS, CSLOTS)], int_sem.at[c])

    for c in range(NCHUNK):
        int_copy(c).start()

    barrier = pltpu.get_barrier_semaphore()
    for other in (left, right):
        pl.semaphore_signal(barrier, inc=1, device_id=(aux, other), device_id_type=MESH)
    pl.semaphore_wait(barrier, 2)
    orb_copy.wait()

    table[512] = jnp.zeros((32, 128), BF16)

    @pl.loop(0, 256, unroll=4)
    def _(k):
        t = orb[:, pl.ds(pl.multiple_of(k * 128, 128), 128)]
        table[k] = t
        table[256 + k] = swap_halves(t.astype(F32)).astype(BF16)

    def part(c, owner):
        return gath.at[c, pl.ds(pl.multiple_of(owner * 32, 32), 32)]

    def send(c, owner, to, ssem, rsem):
        return pltpu.make_async_remote_copy(
            src_ref=part(c, owner), dst_ref=part(c, owner), send_sem=ssem.at[c], recv_sem=rsem.at[c],
            device_id=(aux, to), device_id_type=MESH)

    def to_left(c):
        return send(c, me, left, send_l, recv_r)

    def to_right(c):
        return send(c, me, right, send_r, recv_l)

    def onward(c):
        if c % 2 == 0:
            return send(c, left, right, send_f, recv_f)
        return send(c, right, left, send_f, recv_f)

    for c in range(NCHUNK):
        @pl.loop(0, CSLOTS // 2, unroll=True)
        def _(k, c=c):
            s0 = c * CSLOTS + 2 * k
            lanes = pl.ds(pl.multiple_of(k * 128, 128), 128)
            gath[c, pl.ds(pl.multiple_of(me * 32, 32), 32), lanes] = gather_pair(table, cols[s0], cols[s0 + 1])
        to_left(c).start()
        to_right(c).start()

    for c in range(NCHUNK):
        @pl.loop(0, CSLOTS // 2, unroll=True)
        def _(k, c=c):
            s0 = c * CSLOTS + 2 * k
            lanes = pl.ds(pl.multiple_of(k * 128, 128), 128)
            rbuf[c, :, lanes] = gather_pair(table, rows[s0], rows[s0 + 1])

    facc[...] = jnp.zeros_like(facc)

    def compute(c):
        int_copy(c).wait()

        @pl.loop(0, CSLOTS // 2)
        def _(k):
            lanes = pl.ds(pl.multiple_of(k * 128, 128), 128)
            lhs = gath[c, :, lanes]
            s0 = c * CSLOTS + 2 * k
            low = low_lanes((SIDE, 128))
            for t in range(NAUX // 2):
                a = ints[s0, :, t * 128:(t + 1) * 128].astype(F32)
                b = ints[s0 + 1, :, t * 128:(t + 1) * 128].astype(F32)
                sa, sb = swap_halves(a), swap_halves(b)
                even = jnp.concatenate([jnp.where(low, a, 0.0), jnp.where(low, 0.0, sb)], 0)
                odd = jnp.concatenate([jnp.where(low, sa, 0.0), jnp.where(low, 0.0, b)], 0)
                w = jnp.concatenate([even, odd], 1).astype(BF16)
                h = jnp.dot(lhs, w, preferred_element_type=F32).astype(BF16)
                hbuf[c, 2 * t * 128:(2 * t + 1) * 128, lanes] = h[:, :128]
                hbuf[c, (2 * t + 1) * 128:(2 * t + 2) * 128, lanes] = h[:, 128:]

        @pl.loop(0, NAUX)
        def _(p):
            here = pl.ds(pl.multiple_of(p * 128, 128), 128)
            facc[here, :] += lax.dot_general(
                hbuf[c, here, :], rbuf[c], (((1,), (1,)), ((), ())), preferred_element_type=F32)

    for c in range(NCHUNK):
        to_left(c).wait_recv()
        to_right(c).wait_recv()
        onward(c).start()
        if c > 0:
            onward(c - 1).wait_recv()
            compute(c - 1)
    onward(NCHUNK - 1).wait_recv()
    compute(NCHUNK - 1)

    fit = jnp.transpose(facc[...]).astype(BF16)
    for c in range(NCHUNK):
        out[:, c * CL:(c + 1) * CL] = jnp.dot(fit, hbuf[c], preferred_element_type=F32)
    for c in range(NCHUNK):
        to_left(c).wait_send()
        to_right(c).wait_send()
        onward(c).wait_send()


def applied_slots(cols, rows, integrals, orbitals):
    sem = pltpu.SemaphoreType.DMA
    return pl.pallas_call(
        exchange_kernel,
        out_shape=jax.ShapeDtypeStruct((32, SLOTS * SIDE), F32),
        in_specs=[pl.BlockSpec(memory_space=pltpu.SMEM)] * 2 + [pl.BlockSpec(memory_space=pl.ANY)] * 2,
        out_specs=pl.BlockSpec(memory_space=pltpu.VMEM),
        scratch_shapes=[
            pltpu.VMEM((32, 32768), BF16),
            pltpu.VMEM((513, 32, 128), BF16),
            pltpu.VMEM((SLOTS, SIDE, NAUX * SIDE), BF16),
            pltpu.VMEM((NCHUNK, 128, CL), BF16),
            pltpu.VMEM((NCHUNK, 32, CL), BF16),
            pltpu.VMEM((NCHUNK, NAUX * 128, CL), BF16),
            pltpu.VMEM((NAUX * 128, 32), F32),
            sem, sem((NCHUNK,)),
            sem((NCHUNK,)), sem((NCHUNK,)), sem((NCHUNK,)),
            sem((NCHUNK,)), sem((NCHUNK,)), sem((NCHUNK,)),
        ],
        compiler_params=pltpu.CompilerParams(
            collective_id=0, has_side_effects=True, vmem_limit_bytes=56 * 1024 * 1024),
    )(cols, rows, integrals, orbitals)


def reduce_kernel(inv, prev, terms, out,
                  e2, own, cbuf, crecv, ya, yb, ydl, ydr, ym_l, ym_r, yrl, yrr, yta, ytb, zsend, zrecv, xsend,
                  csend_sem, crecv_sem, ysend_sem, yrecv_sem, zsend_sem, zrecv_sem, xsend_sem, xrecv_sem):
    aux, me = lax.axis_index("aux"), lax.axis_index("occ")
    core = lax.rem(aux, 2)
    z = lax.rem(aux // 2, 8)
    y = aux // 16

    def at(yy, zz, cc):
        return ((yy * 8 + zz) * 2 + cc, me)

    other_core = at(y, z, 1 - core)
    up, down, far = lax.rem(y + 1, 4), lax.rem(y + 3, 4), lax.rem(y + 2, 4)
    dev_up, dev_down = at(up, z, core), at(down, z, core)

    barrier = pltpu.get_barrier_semaphore()
    peers = [other_core, dev_up, dev_down]
    peers += [at(y, lax.rem(z + d, 8), core) for d in range(1, 8)]
    peers += [(aux, lax.rem(me + d, 4)) for d in range(1, 4)]
    for peer in peers:
        pl.semaphore_signal(barrier, inc=1, device_id=peer, device_id_type=MESH)

    e2[SLOTS] = jnp.zeros((32, 128), F32)

    @pl.loop(0, SLOTS // 2)
    def _(k):
        t = terms[:, pl.ds(pl.multiple_of(k * 128, 128), 128)]
        s = swap_halves(t)
        low = low_lanes(t.shape)
        e2[2 * k] = jnp.where(low, t, s) + e2[prev[2 * k]]
        e2[2 * k + 1] = jnp.where(low, s, t) + e2[prev[2 * k + 1]]

    def dense(q):
        a, b = e2[inv[2 * q]], e2[inv[2 * q + 1]]
        return jnp.where(low_lanes(a.shape), a, b)

    pl.semaphore_wait(barrier, 13)

    order = [far, up, down, y]

    def core_copy(n):
        return pltpu.make_async_remote_copy(
            src_ref=cbuf.at[n], dst_ref=crecv.at[n], send_sem=csend_sem.at[n], recv_sem=crecv_sem.at[n],
            device_id=other_core, device_id_type=MESH)

    for n in range(4):
        @pl.loop(0, 32)
        def _(m, n=n):
            q = order[n] * 64 + (m // 4) * 8 + (1 - core) * 4 + m % 4
            cbuf[n, m] = dense(q).astype(BF16)
        core_copy(n).start()

    for n in range(4):
        @pl.loop(0, 32)
        def _(m, n=n):
            q = order[n] * 64 + (m // 4) * 8 + core * 4 + m % 4
            own[n, m] = dense(q)

    def summed(n, m):
        return own[n, m] + crecv[n, m].astype(F32)

    def y_copy(k, src, dst, dev):
        return pltpu.make_async_remote_copy(
            src_ref=src, dst_ref=dst, send_sem=ysend_sem.at[k], recv_sem=yrecv_sem.at[k],
            device_id=dev, device_id_type=MESH)

    t_up = y_copy(0, ya, yta, dev_up)
    t_down = y_copy(1, yb, ytb, dev_down)
    d_up = y_copy(2, ydl, yrl.at[pl.ds(16, 16)], dev_up)
    d_down = y_copy(3, ydr, yrr.at[pl.ds(0, 16)], dev_down)
    m_up = y_copy(4, ym_l, yrl.at[pl.ds(0, 16)], dev_up)
    m_down = y_copy(5, ym_r, yrr.at[pl.ds(16, 16)], dev_down)

    core_copy(0).wait_recv()

    @pl.loop(0, 16)
    def _(m):
        ya[m] = summed(0, m).astype(BF16)
        yb[m] = summed(0, m + 16).astype(BF16)
    t_up.start()
    t_down.start()
    core_copy(1).wait_recv()

    @pl.loop(0, 16)
    def _(m):
        ydl[m] = summed(1, m + 16).astype(BF16)
    d_up.start()
    core_copy(2).wait_recv()

    @pl.loop(0, 16)
    def _(m):
        ydr[m] = summed(2, m).astype(BF16)
    d_down.start()
    t_up.wait_recv()

    @pl.loop(0, 16)
    def _(m):
        ym_l[m] = (summed(1, m) + yta[m].astype(F32)).astype(BF16)
    m_up.start()
    t_down.wait_recv()

    @pl.loop(0, 16)
    def _(m):
        ym_r[m] = (summed(2, m + 16) + ytb[m].astype(F32)).astype(BF16)
    m_down.start()
    core_copy(3).wait_recv()
    d_up.wait_recv()
    d_down.wait_recv()
    m_up.wait_recv()
    m_down.wait_recv()

    @pl.loop(0, 32)
    def _(m):
        v = summed(3, m) + yrl[m].astype(F32) + yrr[m].astype(F32)
        own[3, m] = v
        zsend[m] = v.astype(BF16)

    def z_copy(d):
        to = lax.rem(z + d, 8)
        return pltpu.make_async_remote_copy(
            src_ref=zsend.at[pl.ds(pl.multiple_of(to * 4, 4), 4)], dst_ref=zrecv.at[d - 1],
            send_sem=zsend_sem.at[d - 1], recv_sem=zrecv_sem.at[d - 1],
            device_id=at(y, to, core), device_id_type=MESH)

    for d in (4, 3, 5, 2, 6, 1, 7):
        z_copy(d).start()
    for d in range(1, 8):
        z_copy(d).wait_recv()

    @pl.loop(0, 4)
    def _(m):
        v = own[3, z * 4 + m]
        for d in range(7):
            v = v + zrecv[d, m].astype(F32)
        xsend[m] = v

    here = pl.ds(pl.multiple_of(me * 32, 32), 32)
    out[here, :] = xsend[me]

    def x_copy(d):
        to = lax.rem(me + d, 4)
        return pltpu.make_async_remote_copy(
            src_ref=xsend.at[to], dst_ref=out.at[here],
            send_sem=xsend_sem.at[d - 1], recv_sem=xrecv_sem.at[d - 1],
            device_id=(aux, to), device_id_type=MESH)

    for d in (2, 1, 3):
        x_copy(d).start()
    for n in range(4):
        core_copy(n).wait_send()
    for cp in (t_up, t_down, d_up, d_down, m_up, m_down):
        cp.wait_send()
    for d in range(1, 8):
        z_copy(d).wait_send()
    for d in range(1, 4):
        x_copy(d).wait()


def reduced(inv, prev, terms):
    sem = pltpu.SemaphoreType.DMA
    half = (16, 32, 128)
    return pl.pallas_call(
        reduce_kernel,
        out_shape=jax.ShapeDtypeStruct((128, 128), F32),
        in_specs=[pl.BlockSpec(memory_space=pltpu.SMEM)] * 2 + [pl.BlockSpec(memory_space=pltpu.VMEM)],
        out_specs=pl.BlockSpec(memory_space=pltpu.VMEM),
        scratch_shapes=[
            pltpu.VMEM((SLOTS + 1, 32, 128), F32),
            pltpu.VMEM((4, 32, 32, 128), F32),
            pltpu.VMEM((4, 32, 32, 128), BF16),
            pltpu.VMEM((4, 32, 32, 128), BF16),
            pltpu.VMEM(half, BF16), pltpu.VMEM(half, BF16), pltpu.VMEM(half, BF16), pltpu.VMEM(half, BF16),
            pltpu.VMEM(half, BF16), pltpu.VMEM(half, BF16),
            pltpu.VMEM((32, 32, 128), BF16), pltpu.VMEM((32, 32, 128), BF16),
            pltpu.VMEM(half, BF16), pltpu.VMEM(half, BF16),
            pltpu.VMEM((32, 32, 128), BF16),
            pltpu.VMEM((7, 4, 32, 128), BF16),
            pltpu.VMEM((4, 32, 128), F32),
            sem((4,)), sem((4,)), sem((6,)), sem((6,)), sem((7,)), sem((7,)), sem((3,)), sem((3,)),
        ],
        compiler_params=pltpu.CompilerParams(
            collective_id=1, has_side_effects=True, vmem_limit_bytes=48 * 1024 * 1024),
    )(inv, prev, terms)


def tile_of(block, slot):
    return ((block ^ slot) & 1) * 256 + (block >> 1)


def shards(integrals, slot_row_block, slot_column_block, shard_live_slots, orbitals):
    slot = jnp.arange(SLOTS, dtype=jnp.int32)
    rows = slot_row_block
    hit = rows[None, :] == jnp.arange(512, dtype=jnp.int32)[:, None]
    inv = jnp.max(jnp.where(hit, slot[None, :], -1), axis=1)
    inv = jnp.where(inv < 0, SLOTS, inv)
    same = (rows[None, :] == rows[:, None]) & (slot[None, :] < slot[:, None])
    prev = jnp.max(jnp.where(same, slot[None, :], -1), axis=1)
    prev = jnp.where(prev < 0, SLOTS, prev)
    col_at = jnp.where(slot < shard_live_slots[0], tile_of(slot_column_block, slot), 512)
    terms = applied_slots(col_at, tile_of(rows, slot), integrals, orbitals)
    return reduced(inv, prev, terms)


def solution(mesh):
    placed = (P("aux", None, None), P("aux"), P("aux"), P("aux"), P("occ", None))
    return jax.shard_map(
        shards, mesh=mesh, in_specs=placed, out_specs=P(None, ("aux", "occ")), check_vma=False
    )
```

time: 1570 us -> 104 us (0.07)
  waiting for transfers between devices: 1290 us -> 0 us
  local copies, waits for them, and re-layouts: 170 us -> 1.85 us
  Pallas kernels: 0 us -> 97.9 us
  other arithmetic: 44.5 us -> 2.99 us
  matrix products: 35.4 us -> 0 us
    reduce_scatter x1 -> x0, waiting for transfers between devices: 1290 us -> none  [shards(): lax.psum_scatter(partial_value, ('aux', 'occ'), scatter_dimension=1, tile...]
    pallas_call x0 -> x2, Pallas kernels: none -> 97.9 us  [the longest x1 60.8 us: applied_slots(): pl.pallas_call(exchange_kernel, out_shape=jax.ShapeDtypeStruct((32, SLOTS...]
    dot_general x2 -> x0, local copies, waits for them, and re-layouts: 68.3 us -> none  [shards(): jnp.einsum('pji,rjpx->irx', fitted, split_half, preferred_element_type=jn...]
    reshape x3 -> x0, local copies, waits for them, and re-layouts: 49.6 us -> none  [the longest x1 36.2 us: shards(): split_half = half_done.reshape(block_total, occ_group, aux_here, block_len)]
    dot_general x3 -> x0, matrix products: 35.4 us -> none  [the longest x1 16 us: shards(): jnp.einsum('rjpx,irx->pji', split_half, orb_part, preferred_element_type=...]
    scatter-add x1 -> x0, other arithmetic: 26.9 us -> none  [shards(): jnp.zeros((block_total, occ_group, packed), jnp.float32).at[slot_row_block]]
    convert_element_type x1 -> x0, local copies, waits for them, and re-layouts: 26.3 us -> none  [shards(): half_done = half_done.astype(jnp.bfloat16)]
    convert_element_type x1 -> x0, other arithmetic: 17.6 us -> none  [shards(): half_done = half_done.astype(jnp.bfloat16)]
  transfers between devices with their start and end apart: 2 -> 0, of which waited for: 1 -> 0; matrix products, arithmetic and copies ran while one was open for 14% -> 0% of each run, Pallas kernels for 0% -> 0%
where the time goes in v1:
time: 104 us; the launch traced here: 103 us
  Pallas kernels  97.9 us (94%)
  other arithmetic  2.99 us (3%)
  local copies, waits for them, and re-layouts  1.85 us (2%)
    pallas_call x1, Pallas kernels, applied_slots(): pl.pallas_call(exchange_kernel, out_shape=jax.ShapeDtypeStruct((32, SLOTS...  60.8 us
    pallas_call x1, Pallas kernels, reduced(): pl.pallas_call(reduce_kernel, out_shape=jax.ShapeDtypeStruct((128, 128),...  37 us

profile of v1, /device:TPU:6, one launch (start us, length us, event | category | flops | bytes accessed | tf_op | source)
XLA Modules:
  0.0 103.4 jit_solution(4608365444548249528)
XLA Ops:
  0.7 0.9 select_reduce_fusion.1
  1.6 1.3 %compare_select_fusion.2 = (s32[128]{0:T(128)}, s32[128]{0:T(128)}) fusion(s32[128]{0:T(128)} %param.7, s32[]{:T(128)} %bitcast.1, s32[128]{0:T(128)} %param.6), kind=kLoop, calls=%fused_computation.7 | loop fusion | flops 1536 | bytes 2052 | tf_op jit(solution)/shard_map/jit(_where)/select_n | solution.py:367
  2.8 0.8 select_reduce_fusion
  3.7 60.8 %shard_map.55.terms = f32[32,8192]{1,0:T(8,128)} custom-call(s32[128]{0:T(128)} %get-tuple-element.5.cols, s32[128]{0:T(128)} %get-tuple-element.6.rows, bf16[128,64,512]{2,1,0:T(8,128)(2,1)} %integrals.1, bf16[32,32768]{1,0:T(8,128)(2,1)} %orbitals.1), custom_call_target="tpu_custom_call" | custom-call | tf_op jit(solution)/shard_map/pallas_call | solution.py:147
  64.5 0.0 copy-start
  64.5 1.2 %copy-done = f32[32,8192]{1,0:T(8,128)S(1)} copy-done((f32[32,8192]{1,0:T(8,128)S(1)}, f32[32,8192]{1,0:T(8,128)}, u32[]{:S(2)}) %copy-start) | copy-done | bytes 1048600
  65.7 37.0 %shard_map.56 = f32[128,128]{1,0:T(8,128)S(1)} custom-call(s32[512]{0:T(512)S(1)} %compare_select_fusion.inv, s32[128]{0:T(128)S(1)} %compare_select_fusion.1.prev, f32[32,8192]{1,0:T(8,128)S(1)} %copy-done), custom_call_target="tpu_custom_call" | custom-call | tf_op jit(solution)/shard_map/pallas_call | solution.py:330
  102.8 0.6 copy.8
  (2 shorter events, 0.0 us)
Async XLA Ops:
  64.5 1.2 %copy-start = (f32[32,8192]{1,0:T(8,128)S(1)}, f32[32,8192]{1,0:T(8,128)}, u32[]{:S(2)}) copy-start(f32[32,8192]{1,0:T(8,128)} %shard_map.55.terms) | copy-start | bytes 3145732

commit v2 on v0

v2 whole, which is shorter than its diff:
```python
import jax
import jax.numpy as jnp
from jax import lax
from jax.experimental import pallas as pl
from jax.experimental.pallas import tpu as pltpu
from jax.sharding import PartitionSpec as P

MESH = pl.DeviceIdType.MESH
SLOTS = 128
SIDE = 64
NCHUNK = 8
CSLOTS = SLOTS // NCHUNK
CL = CSLOTS * SIDE
CT = CSLOTS * 128
TILES = 4
F32 = jnp.float32
BF16 = jnp.bfloat16


def swap_halves(v):
    return pltpu.roll(v, SIDE, v.ndim - 1)


def low_lanes(shape):
    return lax.broadcasted_iota(jnp.int32, shape, len(shape) - 1) < SIDE


def lanes_at(k, size):
    return pl.ds(pl.multiple_of(k * size, size), size)


def kernel(col_tile, col_pick, row_tile, row_pick, row_swap, inv, prev, integrals, orbitals, out,
           orb, table, cand, ints, gath, rr, hbuf, facc,
           e2, own, cbuf, crecv, ysend, yfar, yleft, yright, zsend, zrecv, xsend,
           orb_sem, int_sem, send_l, send_r, send_f, recv_l, recv_r, recv_f,
           csend_sem, crecv_sem, ysend_sem, yrecv_sem, zsend_sem, zrecv_sem, xsend_sem, xrecv_sem):
    aux, me = lax.axis_index("aux"), lax.axis_index("occ")
    right, left = lax.rem(me + 1, 4), lax.rem(me + 3, 4)
    core = lax.rem(aux, 2)
    z = lax.rem(aux // 2, 8)
    y = aux // 16

    def at(yy, zz, cc):
        return ((yy * 8 + zz) * 2 + cc, me)

    other_core = at(y, z, 1 - core)
    up, down, far = lax.rem(y + 1, 4), lax.rem(y + 3, 4), lax.rem(y + 2, 4)
    dev_up, dev_down = at(up, z, core), at(down, z, core)

    orb_copy = pltpu.make_async_copy(orbitals, orb, orb_sem)
    orb_copy.start()

    def int_copy(c):
        here = pl.ds(c * CL, CL)
        return pltpu.make_async_copy(integrals.at[here], ints.at[here], int_sem.at[c])

    barrier = pltpu.get_barrier_semaphore()
    peers = [other_core, dev_up, dev_down]
    peers += [at(y, lax.rem(z + d, 8), core) for d in range(1, 8)]
    peers += [(aux, lax.rem(me + d, 4)) for d in range(1, 4)]
    for peer in peers:
        pl.semaphore_signal(barrier, inc=1, device_id=peer, device_id_type=MESH)

    orb_copy.wait()
    for c in range(NCHUNK):
        int_copy(c).start()

    @pl.loop(0, 256, unroll=16)
    def _(k):
        table[k] = orb[:, lanes_at(k, 128)]
    cand[2 * SLOTS] = jnp.zeros((32, 128), BF16)

    def group(c, g):
        return gath.at[c, pl.ds(g * 32, 32)]

    def send(c, g_from, g_to, to, ssem, rsem):
        return pltpu.make_async_remote_copy(
            src_ref=group(c, g_from), dst_ref=group(c, g_to), send_sem=ssem.at[c], recv_sem=rsem.at[c],
            device_id=(aux, to), device_id_type=MESH)

    def to_left(c):
        return send(c, 0, 2, left, send_l, recv_r)

    def to_right(c):
        return send(c, 0, 1, right, send_r, recv_l)

    def onward(c):
        if c % 2 == 0:
            return send(c, 1, 3, right, send_f, recv_f)
        return send(c, 2, 3, left, send_f, recv_f)

    def candidates(tile, c):
        @pl.loop(0, CSLOTS, unroll=8)
        def _(k):
            s = c * CSLOTS + k
            t = table[tile[s]]
            cand[2 * s] = t
            cand[2 * s + 1] = swap_halves(t)

    for c in range(NCHUNK):
        candidates(col_tile, c)

        @pl.loop(0, CSLOTS // 2, unroll=4)
        def _(k, c=c):
            s = c * CSLOTS + 2 * k
            a, b = cand[col_pick[s]], cand[col_pick[s + 1]]
            gath[c, 0:32, lanes_at(k, 128)] = jnp.where(low_lanes(a.shape), a, b)
        if c == 0:
            pl.semaphore_wait(barrier, 13)
        to_left(c).start()
        to_right(c).start()

    for c in range(NCHUNK):
        candidates(row_tile, c)

        @pl.loop(0, CSLOTS, unroll=4)
        def _(k, c=c):
            s = c * CSLOTS + k
            a, b = cand[row_pick[s]], cand[row_swap[s]]
            low = low_lanes(a.shape)
            zero = jnp.zeros_like(a)
            rr[c, 0:32, lanes_at(k, 128)] = jnp.where(low, a, zero)
            rr[c, 32:64, lanes_at(k, 128)] = jnp.where(low, zero, b)

    facc[...] = jnp.zeros_like(facc)

    def half(c, first, count):
        @pl.loop(0, CSLOTS // 2, unroll=2)
        def _(k):
            g = gath[c, first:first + count, lanes_at(k, 128)]
            low = low_lanes(g.shape)
            zero = jnp.zeros_like(g)
            lhs = jnp.concatenate([jnp.where(low, g, zero), jnp.where(low, zero, g)], 0)
            w = ints[lanes_at(c * (CSLOTS // 2) + k, 128), :]
            h = jnp.dot(lhs, w, preferred_element_type=F32).astype(BF16)
            for t in range(TILES):
                for n in range(2):
                    hbuf[c, t * 128 + first:t * 128 + first + count, lanes_at(2 * k + n, 128)] = (
                        h[n * count:(n + 1) * count, t * 128:(t + 1) * 128])

    for c in range(NCHUNK):
        to_left(c).wait_recv()
        to_right(c).wait_recv()
        onward(c).start()
        int_copy(c).wait()
        half(c, 0, 96)
    for c in range(NCHUNK):
        onward(c).wait_recv()
        half(c, 96, 32)
        facc[...] += lax.dot_general(rr[c], hbuf[c], (((1,), (1,)), ((), ())), preferred_element_type=F32)

    fit = facc[...].astype(BF16)
    e2[SLOTS] = jnp.zeros((32, 128), F32)
    for c in range(NCHUNK):
        @pl.loop(0, CSLOTS // 4)
        def _(k, c=c):
            v = jnp.dot(fit, hbuf[c, :, lanes_at(k, 512)], preferred_element_type=F32)
            low = low_lanes((32, 128))
            for n in range(4):
                s = c * CSLOTS + 4 * k + n
                here = slice(n * 128, (n + 1) * 128)
                u = jnp.where(low, v[:32, here], v[32:, here])
                e2[s] = u + swap_halves(u)

    @pl.loop(0, SLOTS, unroll=8)
    def _(s):
        e2[s] = e2[s] + e2[prev[s]]

    order = [far, up, down, y]

    def dense(n, h, m, cc):
        q = order[n] * 64 + (m // 2) * 8 + cc * 4 + 2 * h + m % 2
        a, b = e2[inv[2 * q]], e2[inv[2 * q + 1]]
        return jnp.where(low_lanes(a.shape), a, b)

    def core_copy(n, h):
        k = h * 4 + n
        return pltpu.make_async_remote_copy(
            src_ref=cbuf.at[k], dst_ref=crecv.at[k], send_sem=csend_sem.at[k], recv_sem=crecv_sem.at[k],
            device_id=other_core, device_id_type=MESH)

    for h in range(2):
        for n in range(4):
            @pl.loop(0, 16, unroll=4)
            def _(m, n=n, h=h):
                cbuf[h * 4 + n, m] = dense(n, h, m, 1 - core).astype(BF16)
            core_copy(n, h).start()
    for h in range(2):
        for n in range(4):
            @pl.loop(0, 16, unroll=4)
            def _(m, n=n, h=h):
                own[h * 4 + n, m] = dense(n, h, m, core)

    def summed(n, h, m):
        return own[h * 4 + n, m] + crecv[h * 4 + n, m].astype(F32)

    def y_copy(h, k, dst, dev):
        return pltpu.make_async_remote_copy(
            src_ref=ysend.at[h, k], dst_ref=dst, send_sem=ysend_sem.at[h, k], recv_sem=yrecv_sem.at[h, k],
            device_id=dev, device_id_type=MESH)

    first, last = pl.ds(0, 8), pl.ds(8, 8)

    def y_copies(h):
        return (
            y_copy(h, 0, yfar.at[h, 0], dev_up),
            y_copy(h, 1, yfar.at[h, 1], dev_down),
            y_copy(h, 2, yleft.at[h, last], dev_up),
            y_copy(h, 3, yright.at[h, first], dev_down),
            y_copy(h, 4, yleft.at[h, first], dev_up),
            y_copy(h, 5, yright.at[h, last], dev_down),
        )

    for h in range(2):
        cp = y_copies(h)
        core_copy(0, h).wait_recv()

        @pl.loop(0, 8, unroll=4)
        def _(m, h=h):
            ysend[h, 0, m] = summed(0, h, m).astype(BF16)
            ysend[h, 1, m] = summed(0, h, m + 8).astype(BF16)
        cp[0].start()
        cp[1].start()
        core_copy(1, h).wait_recv()
        core_copy(2, h).wait_recv()

        @pl.loop(0, 8, unroll=4)
        def _(m, h=h):
            ysend[h, 2, m] = summed(1, h, m + 8).astype(BF16)
            ysend[h, 3, m] = summed(2, h, m).astype(BF16)
        cp[2].start()
        cp[3].start()
    for h in range(2):
        cp = y_copies(h)
        cp[0].wait_recv()
        cp[1].wait_recv()

        @pl.loop(0, 8, unroll=4)
        def _(m, h=h):
            ysend[h, 4, m] = (summed(1, h, m) + yfar[h, 0, m].astype(F32)).astype(BF16)
            ysend[h, 5, m] = (summed(2, h, m + 8) + yfar[h, 1, m].astype(F32)).astype(BF16)
        cp[4].start()
        cp[5].start()

    def z_copy(h, d):
        to = lax.rem(z + d, 8)
        return pltpu.make_async_remote_copy(
            src_ref=zsend.at[h, pl.ds(pl.multiple_of(to * 2, 2), 2)], dst_ref=zrecv.at[h, d - 1],
            send_sem=zsend_sem.at[h, d - 1], recv_sem=zrecv_sem.at[h, d - 1],
            device_id=at(y, to, core), device_id_type=MESH)

    for h in range(2):
        core_copy(3, h).wait_recv()
        for cp in y_copies(h)[2:]:
            cp.wait_recv()

        @pl.loop(0, 16, unroll=4)
        def _(m, h=h):
            v = summed(3, h, m) + yleft[h, m].astype(F32) + yright[h, m].astype(F32)
            own[h * 4 + 3, m] = v
            zsend[h, m] = v.astype(BF16)
        for d in (4, 3, 5, 2, 6, 1, 7):
            z_copy(h, d).start()
    for h in range(2):
        for d in range(1, 8):
            z_copy(h, d).wait_recv()
        for m in range(2):
            v = own[h * 4 + 3, z * 2 + m]
            for d in range(7):
                v = v + zrecv[h, d, m].astype(F32)
            xsend[2 * h + m] = v

    here = lanes_at(me, 32)
    out[here, :] = xsend[me]

    def x_copy(d):
        to = lax.rem(me + d, 4)
        return pltpu.make_async_remote_copy(
            src_ref=xsend.at[to], dst_ref=out.at[here],
            send_sem=xsend_sem.at[d - 1], recv_sem=xrecv_sem.at[d - 1],
            device_id=(aux, to), device_id_type=MESH)

    for d in (2, 1, 3):
        x_copy(d).start()
    for c in range(NCHUNK):
        to_left(c).wait_send()
        to_right(c).wait_send()
        onward(c).wait_send()
    for h in range(2):
        for n in range(4):
            core_copy(n, h).wait_send()
        for cp in y_copies(h):
            cp.wait_send()
        for d in range(1, 8):
            z_copy(h, d).wait_send()
    for d in range(1, 4):
        x_copy(d).wait()


def applied(col_tile, col_pick, row_tile, row_pick, row_swap, inv, prev, integrals, orbitals):
    sem = pltpu.SemaphoreType.DMA
    vmem = pltpu.VMEM
    return pl.pallas_call(
        kernel,
        out_shape=jax.ShapeDtypeStruct((128, 128), F32),
        in_specs=[pl.BlockSpec(memory_space=pltpu.SMEM)] * 7 + [pl.BlockSpec(memory_space=pl.ANY)] * 2,
        out_specs=pl.BlockSpec(memory_space=pltpu.VMEM),
        scratch_shapes=[
            vmem((32, 32768), BF16),
            vmem((256, 32, 128), BF16),
            vmem((2 * SLOTS + 1, 32, 128), BF16),
            vmem((SLOTS * SIDE, 512), BF16),
            vmem((NCHUNK, 128, CL), BF16),
            vmem((NCHUNK, 64, CT), BF16),
            vmem((NCHUNK, 512, CT), BF16),
            vmem((64, 512), F32),
            vmem((SLOTS + 1, 32, 128), F32),
            vmem((8, 16, 32, 128), F32),
            vmem((8, 16, 32, 128), BF16),
            vmem((8, 16, 32, 128), BF16),
            vmem((2, 6, 8, 32, 128), BF16),
            vmem((2, 2, 8, 32, 128), BF16),
            vmem((2, 16, 32, 128), BF16),
            vmem((2, 16, 32, 128), BF16),
            vmem((2, 16, 32, 128), BF16),
            vmem((2, 7, 2, 32, 128), BF16),
            vmem((4, 32, 128), F32),
            sem, sem((NCHUNK,)),
            sem((NCHUNK,)), sem((NCHUNK,)), sem((NCHUNK,)),
            sem((NCHUNK,)), sem((NCHUNK,)), sem((NCHUNK,)),
            sem((8,)), sem((8,)), sem((2, 6)), sem((2, 6)), sem((2, 7)), sem((2, 7)), sem((3,)), sem((3,)),
        ],
        compiler_params=pltpu.CompilerParams(
            collective_id=0, has_side_effects=True, vmem_limit_bytes=58 * 1024 * 1024),
    )(col_tile, col_pick, row_tile, row_pick, row_swap, inv, prev, integrals, orbitals)


def shards(integrals, slot_row_block, slot_column_block, shard_live_slots, orbitals):
    slot = jnp.arange(SLOTS, dtype=jnp.int32)
    rows, cols = slot_row_block, slot_column_block
    hit = rows[None, :] == jnp.arange(512, dtype=jnp.int32)[:, None]
    inv = jnp.max(jnp.where(hit, slot[None, :], -1), axis=1)
    inv = jnp.where(inv < 0, SLOTS, inv)
    same = (rows[None, :] == rows[:, None]) & (slot[None, :] < slot[:, None])
    prev = jnp.max(jnp.where(same, slot[None, :], -1), axis=1)
    prev = jnp.where(prev < 0, SLOTS, prev)
    col_pick = jnp.where(slot < shard_live_slots[0], 2 * slot + ((cols ^ slot) & 1), 2 * SLOTS)
    row_pick = 2 * slot + (rows & 1)
    return applied(cols >> 1, col_pick, rows >> 1, row_pick, row_pick ^ 1, inv, prev,
                   integrals.reshape(SLOTS * SIDE, 512), orbitals)


def solution(mesh):
    placed = (P("aux", None, None), P("aux"), P("aux"), P("aux"), P("occ", None))
    return jax.shard_map(
        shards, mesh=mesh, in_specs=placed, out_specs=P(None, ("aux", "occ")), check_vma=False
    )
```

time: 1570 us -> 77 us (0.05)
  waiting for transfers between devices: 1290 us -> 0 us
  local copies, waits for them, and re-layouts: 170 us -> 1.47 us
  Pallas kernels: 0 us -> 69.6 us
  other arithmetic: 44.5 us -> 4.75 us
  matrix products: 35.4 us -> 0 us
    reduce_scatter x1 -> x0, waiting for transfers between devices: 1290 us -> none  [shards(): lax.psum_scatter(partial_value, ('aux', 'occ'), scatter_dimension=1, tile...]
    pallas_call x0 -> x1, Pallas kernels: none -> 69.6 us  [applied(): pl.pallas_call(kernel, out_shape=jax.ShapeDtypeStruct((128, 128), F32), i...]
    dot_general x2 -> x0, local copies, waits for them, and re-layouts: 68.3 us -> none  [shards(): jnp.einsum('pji,rjpx->irx', fitted, split_half, preferred_element_type=jn...]
    reshape x3 -> x0, local copies, waits for them, and re-layouts: 49.6 us -> none  [the longest x1 36.2 us: shards(): split_half = half_done.reshape(block_total, occ_group, aux_here, block_len)]
    dot_general x3 -> x0, matrix products: 35.4 us -> none  [the longest x1 16 us: shards(): jnp.einsum('rjpx,irx->pji', split_half, orb_part, preferred_element_type=...]
    scatter-add x1 -> x0, other arithmetic: 26.9 us -> none  [shards(): jnp.zeros((block_total, occ_group, packed), jnp.float32).at[slot_row_block]]
    convert_element_type x1 -> x0, local copies, waits for them, and re-layouts: 26.3 us -> none  [shards(): half_done = half_done.astype(jnp.bfloat16)]
    convert_element_type x1 -> x0, other arithmetic: 17.6 us -> none  [shards(): half_done = half_done.astype(jnp.bfloat16)]
  transfers between devices with their start and end apart: 2 -> 0, of which waited for: 1 -> 0; matrix products, arithmetic and copies ran while one was open for 14% -> 0% of each run, Pallas kernels for 0% -> 0%
where the time goes in v2:
time: 77 us; the launch traced here: 76.5 us
  Pallas kernels  69.6 us (90%)
  other arithmetic  4.75 us (6%)
  local copies, waits for them, and re-layouts  1.47 us (2%)
    pallas_call x1, Pallas kernels, applied(): pl.pallas_call(kernel, out_shape=jax.ShapeDtypeStruct((128, 128), F32), i...  69.6 us

profile of v2, /device:TPU:6, one launch (start us, length us, event | category | flops | bytes accessed | tf_op | source)
XLA Modules:
  0.0 76.5 jit_solution(9476456257191914712)
XLA Ops:
  0.7 0.9 %select_reduce_fusion.1 = s32[128]{0:T(128)S(1)} fusion(s32[128]{0:T(128)} %param.6), kind=kLoop, calls=%fused_computation.2 | loop fusion | flops 81792 | bytes 1024 | tf_op jit(solution)/shard_map/reduce_max | solution.py:345
  1.6 1.2 %compare_select_fusion.2 = (s32[128]{0:T(128)}, s32[128]{0:T(128)}, s32[128]{0:T(128)}) fusion(s32[128]{0:T(128)} %param.7, s32[]{:T(128)} %bitcast.2, s32[128]{0:T(128)S(1)} %select_reduce_fusion.1), kind=kLoop, calls=%fused_computation.7 | loop fusion | flops 1152 | bytes 2564 | tf_op jit(solution)/shard_map/jit(_where)/select_n | solution.py:347
  2.8 1.3 %broadcast_xor_fusion = (s32[128]{0:T(128)}, s32[128]{0:T(128)}, s32[128]{0:T(128)}) fusion(s32[128]{0:T(128)} %param.6), kind=kLoop, calls=%fused_computation.10 | loop fusion | flops 640 | bytes 2048 | tf_op jit(solution)/shard_map/xor | solution.py:349
  4.0 0.8 %select_reduce_fusion = s32[512]{0:T(512)S(1)} fusion(s32[128]{0:T(128)} %param.6), kind=kLoop, calls=%fused_computation | loop fusion | flops 196096 | bytes 2560 | tf_op jit(solution)/shard_map/reduce_max | solution.py:342
  4.8 0.6 compare_select_fusion.inv
  5.4 69.6 %shard_map.55 = f32[128,128]{1,0:T(8,128)} custom-call(s32[128]{0:T(128)} %get-tuple-element.9.col_tile, s32[128]{0:T(128)} %get-tuple-element.8.col_pick, s32[128]{0:T(128)} %get-tuple-element.7.row_tile, s32[128]{0:T(128)} %get-tuple-element.6.row_pick, s32[128]{0:T(128)} %get-tuple-element.5.row_swap, s32[512]{0:T(512)} %compare_select_fusion.inv, ...), custom_call_target="tpu_custom_call" | custom-call | tf_op jit(solution)/shard_map/pallas_call | solution.py:303
  75.0 1.5 %copy.8 = f32[128,128]{1,0:T(8,128)} copy(f32[128,128]{1,0:T(8,128)} %shard_map.55) | data formatting | bytes 131072

commit v3 on v2

--- a/solution.py
+++ b/solution.py
@@ -29,10 +29,10 @@
     return pl.ds(pl.multiple_of(k * size, size), size)
 
 
-def kernel(col_tile, col_pick, row_tile, row_pick, row_swap, inv, prev, integrals, orbitals, out,
-           orb, table, cand, ints, gath, rr, hbuf, facc,
+def kernel(cols, rows, live, row_lanes, integrals, orbitals, out,
+           orb, table, lists, maps, ints, gath, rr, hbuf, facc,
            e2, own, cbuf, crecv, ysend, yfar, yleft, yright, zsend, zrecv, xsend,
-           orb_sem, int_sem, send_l, send_r, send_f, recv_l, recv_r, recv_f,
+           orb_sem, map_sem, int_sem, send_l, send_r, send_f, recv_l, recv_r, recv_f,
            csend_sem, crecv_sem, ysend_sem, yrecv_sem, zsend_sem, zrecv_sem, xsend_sem, xrecv_sem):
     aux, me = lax.axis_index("aux"), lax.axis_index("occ")
     right, left = lax.rem(me + 1, 4), lax.rem(me + 3, 4)
@@ -61,14 +61,31 @@
     for peer in peers:
         pl.semaphore_signal(barrier, inc=1, device_id=peer, device_id_type=MESH)
 
+    across = jnp.broadcast_to(row_lanes[...], (SLOTS, 128))
+    along = jnp.transpose(across)
+    slot = lax.broadcasted_iota(jnp.int32, (SLOTS, 128), 0)
+    lane = lax.broadcasted_iota(jnp.int32, (SLOTS, 128), 1)
+
+    def last_of(hit):
+        v = jnp.max(jnp.where(hit, slot, -1), axis=0, keepdims=True)
+        return jnp.where(v < 0, SLOTS, v)
+
+    for r in range(4):
+        lists[r:r + 1, :] = last_of(along == lane + r * 128)
+    lists[4:5, :] = last_of((along == across) & (slot < lane))
+    lists[5:8, :] = jnp.full((3, 128), SLOTS, jnp.int32)
+    map_copy = pltpu.make_async_copy(lists, maps, map_sem)
+    map_copy.start()
+
     orb_copy.wait()
     for c in range(NCHUNK):
         int_copy(c).start()
 
-    @pl.loop(0, 256, unroll=16)
+    table[256] = jnp.zeros((32, 128), BF16)
+
+    @pl.loop(0, 256, unroll=32)
     def _(k):
         table[k] = orb[:, lanes_at(k, 128)]
-    cand[2 * SLOTS] = jnp.zeros((32, 128), BF16)
 
     def group(c, g):
         return gath.at[c, pl.ds(g * 32, 32)]
@@ -89,43 +106,38 @@
             return send(c, 1, 3, right, send_f, recv_f)
         return send(c, 2, 3, left, send_f, recv_f)
 
-    def candidates(tile, c):
-        @pl.loop(0, CSLOTS, unroll=8)
-        def _(k):
-            s = c * CSLOTS + k
-            t = table[tile[s]]
-            cand[2 * s] = t
-            cand[2 * s + 1] = swap_halves(t)
-
-    for c in range(NCHUNK):
-        candidates(col_tile, c)
-
-        @pl.loop(0, CSLOTS // 2, unroll=4)
-        def _(k, c=c):
+    count = live[0]
+
+    def column(s, half):
+        b = cols[s]
+        alive = jnp.minimum(jnp.maximum(count - s, 0), 1)
+        return pltpu.roll(table[256 + ((b >> 1) - 256) * alive], ((b ^ half) & 1) * SIDE, 1)
+
+    for c in range(NCHUNK):
+        for k in range(CSLOTS // 2):
             s = c * CSLOTS + 2 * k
-            a, b = cand[col_pick[s]], cand[col_pick[s + 1]]
-            gath[c, 0:32, lanes_at(k, 128)] = jnp.where(low_lanes(a.shape), a, b)
+            a, b = column(s, 0), column(s + 1, 1)
+            gath[c, 0:32, k * 128:(k + 1) * 128] = jnp.where(low_lanes(a.shape), a, b)
         if c == 0:
             pl.semaphore_wait(barrier, 13)
         to_left(c).start()
         to_right(c).start()
 
     for c in range(NCHUNK):
-        candidates(row_tile, c)
-
-        @pl.loop(0, CSLOTS, unroll=4)
+        @pl.loop(0, CSLOTS, unroll=CSLOTS)
         def _(k, c=c):
-            s = c * CSLOTS + k
-            a, b = cand[row_pick[s]], cand[row_swap[s]]
+            b = rows[c * CSLOTS + k]
+            t = table[b >> 1]
+            a = pltpu.roll(t, (b & 1) * SIDE, 1)
             low = low_lanes(a.shape)
             zero = jnp.zeros_like(a)
             rr[c, 0:32, lanes_at(k, 128)] = jnp.where(low, a, zero)
-            rr[c, 32:64, lanes_at(k, 128)] = jnp.where(low, zero, b)
+            rr[c, 32:64, lanes_at(k, 128)] = jnp.where(low, zero, swap_halves(a))
 
     facc[...] = jnp.zeros_like(facc)
 
     def half(c, first, count):
-        @pl.loop(0, CSLOTS // 2, unroll=2)
+        @pl.loop(0, CSLOTS // 2, unroll=8)
         def _(k):
             g = gath[c, first:first + count, lanes_at(k, 128)]
             low = low_lanes(g.shape)
@@ -150,9 +162,10 @@
         facc[...] += lax.dot_general(rr[c], hbuf[c], (((1,), (1,)), ((), ())), preferred_element_type=F32)
 
     fit = facc[...].astype(BF16)
+    map_copy.wait()
     e2[SLOTS] = jnp.zeros((32, 128), F32)
     for c in range(NCHUNK):
-        @pl.loop(0, CSLOTS // 4)
+        @pl.loop(0, CSLOTS // 4, unroll=4)
         def _(k, c=c):
             v = jnp.dot(fit, hbuf[c, :, lanes_at(k, 512)], preferred_element_type=F32)
             low = low_lanes((32, 128))
@@ -160,17 +173,13 @@
                 s = c * CSLOTS + 4 * k + n
                 here = slice(n * 128, (n + 1) * 128)
                 u = jnp.where(low, v[:32, here], v[32:, here])
-                e2[s] = u + swap_halves(u)
-
-    @pl.loop(0, SLOTS, unroll=8)
-    def _(s):
-        e2[s] = e2[s] + e2[prev[s]]
+                e2[s] = u + swap_halves(u) + e2[maps[4, s]]
 
     order = [far, up, down, y]
 
     def dense(n, h, m, cc):
-        q = order[n] * 64 + (m // 2) * 8 + cc * 4 + 2 * h + m % 2
-        a, b = e2[inv[2 * q]], e2[inv[2 * q + 1]]
+        row, col = order[n], 2 * ((m // 2) * 8 + cc * 4 + 2 * h + m % 2)
+        a, b = e2[maps[row, col]], e2[maps[row, col + 1]]
         return jnp.where(low_lanes(a.shape), a, b)
 
     def core_copy(n, h):
@@ -181,13 +190,13 @@
 
     for h in range(2):
         for n in range(4):
-            @pl.loop(0, 16, unroll=4)
+            @pl.loop(0, 16, unroll=16)
             def _(m, n=n, h=h):
                 cbuf[h * 4 + n, m] = dense(n, h, m, 1 - core).astype(BF16)
             core_copy(n, h).start()
     for h in range(2):
         for n in range(4):
-            @pl.loop(0, 16, unroll=4)
+            @pl.loop(0, 16, unroll=16)
             def _(m, n=n, h=h):
                 own[h * 4 + n, m] = dense(n, h, m, core)
 
@@ -215,7 +224,7 @@
         cp = y_copies(h)
         core_copy(0, h).wait_recv()
 
-        @pl.loop(0, 8, unroll=4)
+        @pl.loop(0, 8, unroll=8)
         def _(m, h=h):
             ysend[h, 0, m] = summed(0, h, m).astype(BF16)
             ysend[h, 1, m] = summed(0, h, m + 8).astype(BF16)
@@ -224,7 +233,7 @@
         core_copy(1, h).wait_recv()
         core_copy(2, h).wait_recv()
 
-        @pl.loop(0, 8, unroll=4)
+        @pl.loop(0, 8, unroll=8)
         def _(m, h=h):
             ysend[h, 2, m] = summed(1, h, m + 8).astype(BF16)
             ysend[h, 3, m] = summed(2, h, m).astype(BF16)
@@ -235,7 +244,7 @@
         cp[0].wait_recv()
         cp[1].wait_recv()
 
-        @pl.loop(0, 8, unroll=4)
+        @pl.loop(0, 8, unroll=8)
         def _(m, h=h):
             ysend[h, 4, m] = (summed(1, h, m) + yfar[h, 0, m].astype(F32)).astype(BF16)
             ysend[h, 5, m] = (summed(2, h, m + 8) + yfar[h, 1, m].astype(F32)).astype(BF16)
@@ -254,7 +263,7 @@
         for cp in y_copies(h)[2:]:
             cp.wait_recv()
 
-        @pl.loop(0, 16, unroll=4)
+        @pl.loop(0, 16, unroll=16)
         def _(m, h=h):
             v = summed(3, h, m) + yleft[h, m].astype(F32) + yright[h, m].astype(F32)
             own[h * 4 + 3, m] = v
@@ -297,18 +306,20 @@
         x_copy(d).wait()
 
 
-def applied(col_tile, col_pick, row_tile, row_pick, row_swap, inv, prev, integrals, orbitals):
+def applied(cols, rows, live, row_lanes, integrals, orbitals):
     sem = pltpu.SemaphoreType.DMA
     vmem = pltpu.VMEM
     return pl.pallas_call(
         kernel,
         out_shape=jax.ShapeDtypeStruct((128, 128), F32),
-        in_specs=[pl.BlockSpec(memory_space=pltpu.SMEM)] * 7 + [pl.BlockSpec(memory_space=pl.ANY)] * 2,
+        in_specs=[pl.BlockSpec(memory_space=pltpu.SMEM)] * 3 + [pl.BlockSpec(memory_space=pltpu.VMEM)]
+        + [pl.BlockSpec(memory_space=pl.ANY)] * 2,
         out_specs=pl.BlockSpec(memory_space=pltpu.VMEM),
         scratch_shapes=[
             vmem((32, 32768), BF16),
-            vmem((256, 32, 128), BF16),
-            vmem((2 * SLOTS + 1, 32, 128), BF16),
+            vmem((257, 32, 128), BF16),
+            vmem((8, 128), jnp.int32),
+            pltpu.SMEM((8, 128), jnp.int32),
             vmem((SLOTS * SIDE, 512), BF16),
             vmem((NCHUNK, 128, CL), BF16),
             vmem((NCHUNK, 64, CT), BF16),
@@ -325,28 +336,18 @@
             vmem((2, 16, 32, 128), BF16),
             vmem((2, 7, 2, 32, 128), BF16),
             vmem((4, 32, 128), F32),
-            sem, sem((NCHUNK,)),
+            sem, sem, sem((NCHUNK,)),
             sem((NCHUNK,)), sem((NCHUNK,)), sem((NCHUNK,)),
             sem((NCHUNK,)), sem((NCHUNK,)), sem((NCHUNK,)),
             sem((8,)), sem((8,)), sem((2, 6)), sem((2, 6)), sem((2, 7)), sem((2, 7)), sem((3,)), sem((3,)),
         ],
         compiler_params=pltpu.CompilerParams(
             collective_id=0, has_side_effects=True, vmem_limit_bytes=58 * 1024 * 1024),
-    )(col_tile, col_pick, row_tile, row_pick, row_swap, inv, prev, integrals, orbitals)
+    )(cols, rows, live, row_lanes, integrals, orbitals)
 
 
 def shards(integrals, slot_row_block, slot_column_block, shard_live_slots, orbitals):
-    slot = jnp.arange(SLOTS, dtype=jnp.int32)
-    rows, cols = slot_row_block, slot_column_block
-    hit = rows[None, :] == jnp.arange(512, dtype=jnp.int32)[:, None]
-    inv = jnp.max(jnp.where(hit, slot[None, :], -1), axis=1)
-    inv = jnp.where(inv < 0, SLOTS, inv)
-    same = (rows[None, :] == rows[:, None]) & (slot[None, :] < slot[:, None])
-    prev = jnp.max(jnp.where(same, slot[None, :], -1), axis=1)
-    prev = jnp.where(prev < 0, SLOTS, prev)
-    col_pick = jnp.where(slot < shard_live_slots[0], 2 * slot + ((cols ^ slot) & 1), 2 * SLOTS)
-    row_pick = 2 * slot + (rows & 1)
-    return applied(cols >> 1, col_pick, rows >> 1, row_pick, row_pick ^ 1, inv, prev,
+    return applied(slot_column_block, slot_row_block, shard_live_slots, slot_row_block.reshape(1, SLOTS),
                    integrals.reshape(SLOTS * SIDE, 512), orbitals)
 
 

time: 77 us -> 61.4 us (0.80)
  Pallas kernels: 69.6 us -> 58.9 us
  other arithmetic: 4.75 us -> 0 us
    pallas_call x1, Pallas kernels: 69.6 us -> 58.9 us  [applied(): pl.pallas_call(kernel, out_shape=jax.ShapeDtypeStruct((128, 128), F32), i...]
    select_n x2 -> x0, other arithmetic: 1.79 us -> none  [the longest x1 1.21 us: shards(): jnp.where(slot < shard_live_slots[0], 2 * slot + ((cols ^ slot) & 1), 2 *...]
    reduce_max x2 -> x0, other arithmetic: 1.71 us -> none  [the longest x1 0.91 us: shards(): prev = jnp.max(jnp.where(same, slot[None, :], -1), axis=1)]
    xor x1 -> x0, other arithmetic: 1.25 us -> none  [shards(): row_pick ^ 1]
where the time goes in v3:
time: 61.4 us; the launch traced here: 61 us
  Pallas kernels  58.9 us (96%)
  local copies, waits for them, and re-layouts  1.47 us (2%)
  between operations  0.66 us (1%)
    pallas_call x1, Pallas kernels, applied(): pl.pallas_call(kernel, out_shape=jax.ShapeDtypeStruct((128, 128), F32), i...  58.9 us
    unnamed x1, local copies, waits for them, and re-layouts  1.47 us

profile of v3, /device:TPU:6, one launch (start us, length us, event | category | flops | bytes accessed | tf_op | source)
XLA Modules:
  0.0 61.0 jit_solution(11256268572340454102)
XLA Ops:
  0.7 58.9 %shard_map.55 = f32[128,128]{1,0:T(8,128)} custom-call(s32[128]{0:T(128)} %cols.1, s32[128]{0:T(128)} %rows.1, s32[1]{0:T(128)S(6)} %copy.7.live, s32[1,128]{1,0:T(1,128)} %bitcast.3, bf16[8192,512]{1,0:T(8,128)(2,1)} %bitcast.2, bf16[32,32768]{1,0:T(8,128)(2,1)} %orbitals.1), custom_call_target="tpu_custom_call" | custom-call | tf_op jit(solution)/shard_map/pallas_call | solution.py:312
  59.6 1.5 %copy.8 = f32[128,128]{1,0:T(8,128)} copy(f32[128,128]{1,0:T(8,128)} %shard_map.55) | data formatting | bytes 131072

commit v4 on v3

--- a/solution.py
+++ b/solution.py
@@ -114,25 +114,25 @@
         return pltpu.roll(table[256 + ((b >> 1) - 256) * alive], ((b ^ half) & 1) * SIDE, 1)
 
     for c in range(NCHUNK):
+        found = [column(c * CSLOTS + k, k % 2) for k in range(CSLOTS)]
+        low = low_lanes((32, 128))
         for k in range(CSLOTS // 2):
-            s = c * CSLOTS + 2 * k
-            a, b = column(s, 0), column(s + 1, 1)
-            gath[c, 0:32, k * 128:(k + 1) * 128] = jnp.where(low_lanes(a.shape), a, b)
+            gath[c, 0:32, k * 128:(k + 1) * 128] = jnp.where(low, found[2 * k], found[2 * k + 1])
         if c == 0:
             pl.semaphore_wait(barrier, 13)
         to_left(c).start()
         to_right(c).start()
 
     for c in range(NCHUNK):
-        @pl.loop(0, CSLOTS, unroll=CSLOTS)
-        def _(k, c=c):
-            b = rows[c * CSLOTS + k]
-            t = table[b >> 1]
-            a = pltpu.roll(t, (b & 1) * SIDE, 1)
-            low = low_lanes(a.shape)
-            zero = jnp.zeros_like(a)
-            rr[c, 0:32, lanes_at(k, 128)] = jnp.where(low, a, zero)
-            rr[c, 32:64, lanes_at(k, 128)] = jnp.where(low, zero, swap_halves(a))
+        blocks = [rows[c * CSLOTS + k] for k in range(CSLOTS)]
+        tiles = [table[b >> 1] for b in blocks]
+        low = low_lanes((32, 128))
+        zero = jnp.zeros((32, 128), BF16)
+        in_low = [jnp.where(low, pltpu.roll(t, (b & 1) * SIDE, 1), zero) for b, t in zip(blocks, tiles)]
+        in_high = [jnp.where(low, zero, pltpu.roll(t, ((b & 1) ^ 1) * SIDE, 1)) for b, t in zip(blocks, tiles)]
+        for k in range(CSLOTS):
+            rr[c, 0:32, k * 128:(k + 1) * 128] = in_low[k]
+            rr[c, 32:64, k * 128:(k + 1) * 128] = in_high[k]
 
     facc[...] = jnp.zeros_like(facc)
 
@@ -177,10 +177,11 @@
 
     order = [far, up, down, y]
 
-    def dense(n, h, m, cc):
-        row, col = order[n], 2 * ((m // 2) * 8 + cc * 4 + 2 * h + m % 2)
-        a, b = e2[maps[row, col]], e2[maps[row, col + 1]]
-        return jnp.where(low_lanes(a.shape), a, b)
+    def dense(n, h, first, cc):
+        low = low_lanes((32, 128))
+        spots = [2 * ((first + m) // 2 * 8 + cc * 4 + 2 * h + m % 2) for m in range(8)]
+        pairs = [(e2[maps[order[n], at]], e2[maps[order[n], at + 1]]) for at in spots]
+        return [jnp.where(low, a, b) for a, b in pairs]
 
     def core_copy(n, h):
         k = h * 4 + n
@@ -188,20 +189,14 @@
             src_ref=cbuf.at[k], dst_ref=crecv.at[k], send_sem=csend_sem.at[k], recv_sem=crecv_sem.at[k],
             device_id=other_core, device_id_type=MESH)
 
-    for h in range(2):
-        for n in range(4):
-            @pl.loop(0, 16, unroll=16)
-            def _(m, n=n, h=h):
-                cbuf[h * 4 + n, m] = dense(n, h, m, 1 - core).astype(BF16)
-            core_copy(n, h).start()
-    for h in range(2):
-        for n in range(4):
-            @pl.loop(0, 16, unroll=16)
-            def _(m, n=n, h=h):
-                own[h * 4 + n, m] = dense(n, h, m, core)
-
-    def summed(n, h, m):
-        return own[h * 4 + n, m] + crecv[h * 4 + n, m].astype(F32)
+    def share(n, h):
+        for first in (0, 8):
+            for m, v in enumerate(dense(n, h, first, 1 - core)):
+                cbuf[h * 4 + n, first + m] = v.astype(BF16)
+        core_copy(n, h).start()
+
+    def summed(n, h, first):
+        return [v + crecv[h * 4 + n, first + m].astype(F32) for m, v in enumerate(dense(n, h, first, core))]
 
     def y_copy(h, k, dst, dev):
         return pltpu.make_async_remote_copy(
@@ -220,36 +215,43 @@
             y_copy(h, 5, yright.at[h, last], dev_down),
         )
 
-    for h in range(2):
-        cp = y_copies(h)
+    def fill(h, k, values):
+        for m, v in enumerate(values):
+            ysend[h, k, m] = v.astype(BF16)
+        y_copies(h)[k].start()
+
+    def send_far(h):
         core_copy(0, h).wait_recv()
-
-        @pl.loop(0, 8, unroll=8)
-        def _(m, h=h):
-            ysend[h, 0, m] = summed(0, h, m).astype(BF16)
-            ysend[h, 1, m] = summed(0, h, m + 8).astype(BF16)
-        cp[0].start()
-        cp[1].start()
+        fill(h, 0, summed(0, h, 0))
+        fill(h, 1, summed(0, h, 8))
+
+    def send_near(h):
         core_copy(1, h).wait_recv()
+        fill(h, 2, summed(1, h, 8))
         core_copy(2, h).wait_recv()
-
-        @pl.loop(0, 8, unroll=8)
-        def _(m, h=h):
-            ysend[h, 2, m] = summed(1, h, m + 8).astype(BF16)
-            ysend[h, 3, m] = summed(2, h, m).astype(BF16)
-        cp[2].start()
-        cp[3].start()
-    for h in range(2):
+        fill(h, 3, summed(2, h, 0))
+
+    def send_merged(h):
         cp = y_copies(h)
         cp[0].wait_recv()
+        fill(h, 4, [v + yfar[h, 0, m].astype(F32) for m, v in enumerate(summed(1, h, 0))])
         cp[1].wait_recv()
-
-        @pl.loop(0, 8, unroll=8)
-        def _(m, h=h):
-            ysend[h, 4, m] = (summed(1, h, m) + yfar[h, 0, m].astype(F32)).astype(BF16)
-            ysend[h, 5, m] = (summed(2, h, m + 8) + yfar[h, 1, m].astype(F32)).astype(BF16)
-        cp[4].start()
-        cp[5].start()
+        fill(h, 5, [v + yfar[h, 1, m].astype(F32) for m, v in enumerate(summed(2, h, 8))])
+
+    share(0, 0)
+    share(1, 0)
+    share(2, 0)
+    share(0, 1)
+    send_far(0)
+    send_near(0)
+    share(1, 1)
+    share(2, 1)
+    send_far(1)
+    send_merged(0)
+    send_near(1)
+    share(3, 0)
+    share(3, 1)
+    send_merged(1)
 
     def z_copy(h, d):
         to = lax.rem(z + d, 8)
@@ -263,18 +265,18 @@
         for cp in y_copies(h)[2:]:
             cp.wait_recv()
 
-        @pl.loop(0, 16, unroll=16)
-        def _(m, h=h):
-            v = summed(3, h, m) + yleft[h, m].astype(F32) + yright[h, m].astype(F32)
-            own[h * 4 + 3, m] = v
-            zsend[h, m] = v.astype(BF16)
+        for base in (0, 8):
+            for m, v in enumerate(summed(3, h, base), base):
+                v = v + yleft[h, m].astype(F32) + yright[h, m].astype(F32)
+                own[h, m] = v
+                zsend[h, m] = v.astype(BF16)
         for d in (4, 3, 5, 2, 6, 1, 7):
             z_copy(h, d).start()
     for h in range(2):
         for d in range(1, 8):
             z_copy(h, d).wait_recv()
         for m in range(2):
-            v = own[h * 4 + 3, z * 2 + m]
+            v = own[h, z * 2 + m]
             for d in range(7):
                 v = v + zrecv[h, d, m].astype(F32)
             xsend[2 * h + m] = v
@@ -326,7 +328,7 @@
             vmem((NCHUNK, 512, CT), BF16),
             vmem((64, 512), F32),
             vmem((SLOTS + 1, 32, 128), F32),
-            vmem((8, 16, 32, 128), F32),
+            vmem((2, 16, 32, 128), F32),
             vmem((8, 16, 32, 128), BF16),
             vmem((8, 16, 32, 128), BF16),
             vmem((2, 6, 8, 32, 128), BF16),

time: 61.4 us -> 60.5 us (0.985)
  Pallas kernels: 58.9 us -> 57.5 us
    pallas_call x1, Pallas kernels: 58.9 us -> 57.5 us  [applied(): pl.pallas_call(kernel, out_shape=jax.ShapeDtypeStruct((128, 128), F32), i...]
where the time goes in v4:
time: 60.5 us; the launch traced here: 59.7 us
  Pallas kernels  57.5 us (95%)
  local copies, waits for them, and re-layouts  1.47 us (2%)
  between operations  0.66 us (1%)
    pallas_call x1, Pallas kernels, applied(): pl.pallas_call(kernel, out_shape=jax.ShapeDtypeStruct((128, 128), F32), i...  57.5 us
    unnamed x1, local copies, waits for them, and re-layouts  1.47 us

profile of v4, /device:TPU:6, one launch (start us, length us, event | category | flops | bytes accessed | tf_op | source)
XLA Modules:
  0.0 59.7 jit_solution(8110739749757854152)
XLA Ops:
  0.7 57.5 %shard_map.55 = f32[128,128]{1,0:T(8,128)} custom-call(s32[128]{0:T(128)} %cols.1, s32[128]{0:T(128)} %rows.1, s32[1]{0:T(128)S(6)} %copy.7.live, s32[1,128]{1,0:T(1,128)} %bitcast.3, bf16[8192,512]{1,0:T(8,128)(2,1)} %bitcast.2, bf16[32,32768]{1,0:T(8,128)(2,1)} %orbitals.1), custom_call_target="tpu_custom_call" | custom-call | tf_op jit(solution)/shard_map/pallas_call | solution.py:314
  58.2 1.5 %copy.8 = f32[128,128]{1,0:T(8,128)} copy(f32[128,128]{1,0:T(8,128)} %shard_map.55) | data formatting | bytes 131072

commit v5 on v4

--- a/solution.py
+++ b/solution.py
@@ -137,6 +137,8 @@
     facc[...] = jnp.zeros_like(facc)
 
     def half(c, first, count):
+        base = 4 * first
+
         @pl.loop(0, CSLOTS // 2, unroll=8)
         def _(k):
             g = gath[c, first:first + count, lanes_at(k, 128)]
@@ -147,8 +149,11 @@
             h = jnp.dot(lhs, w, preferred_element_type=F32).astype(BF16)
             for t in range(TILES):
                 for n in range(2):
-                    hbuf[c, t * 128 + first:t * 128 + first + count, lanes_at(2 * k + n, 128)] = (
+                    hbuf[c, base + t * count:base + (t + 1) * count, lanes_at(2 * k + n, 128)] = (
                         h[n * count:(n + 1) * count, t * 128:(t + 1) * 128])
+        rows_here = slice(base, base + 4 * count)
+        facc[:, rows_here] += lax.dot_general(
+            rr[c], hbuf[c, rows_here, :], (((1,), (1,)), ((), ())), preferred_element_type=F32)
 
     for c in range(NCHUNK):
         to_left(c).wait_recv()
@@ -159,7 +164,6 @@
     for c in range(NCHUNK):
         onward(c).wait_recv()
         half(c, 96, 32)
-        facc[...] += lax.dot_general(rr[c], hbuf[c], (((1,), (1,)), ((), ())), preferred_element_type=F32)
 
     fit = facc[...].astype(BF16)
     map_copy.wait()
@@ -176,11 +180,12 @@
                 e2[s] = u + swap_halves(u) + e2[maps[4, s]]
 
     order = [far, up, down, y]
-
-    def dense(n, h, first, cc):
+    owner = [lax.rem(me + d, 4) for d in (2, 1, 3)] + [me]
+
+    def dense(n, h, first, count, cc):
         low = low_lanes((32, 128))
-        spots = [2 * ((first + m) // 2 * 8 + cc * 4 + 2 * h + m % 2) for m in range(8)]
-        pairs = [(e2[maps[order[n], at]], e2[maps[order[n], at + 1]]) for at in spots]
+        spots = [2 * ((first + m) * 8 + cc * 4 + owner[h]) for m in range(count)]
+        pairs = [(e2[maps[order[n], spot]], e2[maps[order[n], spot + 1]]) for spot in spots]
         return [jnp.where(low, a, b) for a, b in pairs]
 
     def core_copy(n, h):
@@ -190,122 +195,118 @@
             device_id=other_core, device_id_type=MESH)
 
     def share(n, h):
-        for first in (0, 8):
-            for m, v in enumerate(dense(n, h, first, 1 - core)):
-                cbuf[h * 4 + n, first + m] = v.astype(BF16)
+        for m, v in enumerate(dense(n, h, 0, 8, 1 - core)):
+            cbuf[h * 4 + n, m] = v.astype(BF16)
         core_copy(n, h).start()
 
-    def summed(n, h, first):
-        return [v + crecv[h * 4 + n, first + m].astype(F32) for m, v in enumerate(dense(n, h, first, core))]
-
-    def y_copy(h, k, dst, dev):
+    def summed(n, h, first, count):
+        found = dense(n, h, first, count, core)
+        return [v + crecv[h * 4 + n, first + m].astype(F32) for m, v in enumerate(found)]
+
+    def y_copy(h, k):
+        near, away = pl.ds(0, 4), pl.ds(4, 4)
+        dst = (yfar.at[h, 0], yfar.at[h, 1], yleft.at[h, away], yright.at[h, near],
+               yleft.at[h, near], yright.at[h, away])[k]
         return pltpu.make_async_remote_copy(
             src_ref=ysend.at[h, k], dst_ref=dst, send_sem=ysend_sem.at[h, k], recv_sem=yrecv_sem.at[h, k],
-            device_id=dev, device_id_type=MESH)
-
-    first, last = pl.ds(0, 8), pl.ds(8, 8)
-
-    def y_copies(h):
-        return (
-            y_copy(h, 0, yfar.at[h, 0], dev_up),
-            y_copy(h, 1, yfar.at[h, 1], dev_down),
-            y_copy(h, 2, yleft.at[h, last], dev_up),
-            y_copy(h, 3, yright.at[h, first], dev_down),
-            y_copy(h, 4, yleft.at[h, first], dev_up),
-            y_copy(h, 5, yright.at[h, last], dev_down),
-        )
+            device_id=dev_down if k % 2 else dev_up, device_id_type=MESH)
 
     def fill(h, k, values):
         for m, v in enumerate(values):
             ysend[h, k, m] = v.astype(BF16)
-        y_copies(h)[k].start()
-
-    def send_far(h):
+        y_copy(h, k).start()
+
+    def send_direct(h):
         core_copy(0, h).wait_recv()
-        fill(h, 0, summed(0, h, 0))
-        fill(h, 1, summed(0, h, 8))
-
-    def send_near(h):
+        fill(h, 0, summed(0, h, 0, 4))
+        fill(h, 1, summed(0, h, 4, 4))
         core_copy(1, h).wait_recv()
-        fill(h, 2, summed(1, h, 8))
+        fill(h, 2, summed(1, h, 4, 4))
         core_copy(2, h).wait_recv()
-        fill(h, 3, summed(2, h, 0))
+        fill(h, 3, summed(2, h, 0, 4))
 
     def send_merged(h):
-        cp = y_copies(h)
-        cp[0].wait_recv()
-        fill(h, 4, [v + yfar[h, 0, m].astype(F32) for m, v in enumerate(summed(1, h, 0))])
-        cp[1].wait_recv()
-        fill(h, 5, [v + yfar[h, 1, m].astype(F32) for m, v in enumerate(summed(2, h, 8))])
-
-    share(0, 0)
-    share(1, 0)
-    share(2, 0)
-    share(0, 1)
-    send_far(0)
-    send_near(0)
-    share(1, 1)
-    share(2, 1)
-    send_far(1)
-    send_merged(0)
-    send_near(1)
-    share(3, 0)
-    share(3, 1)
-    send_merged(1)
+        y_copy(h, 0).wait_recv()
+        fill(h, 4, [v + yfar[h, 0, m].astype(F32) for m, v in enumerate(summed(1, h, 0, 4))])
+        y_copy(h, 1).wait_recv()
+        fill(h, 5, [v + yfar[h, 1, m].astype(F32) for m, v in enumerate(summed(2, h, 4, 4))])
 
     def z_copy(h, d):
         to = lax.rem(z + d, 8)
         return pltpu.make_async_remote_copy(
-            src_ref=zsend.at[h, pl.ds(pl.multiple_of(to * 2, 2), 2)], dst_ref=zrecv.at[h, d - 1],
+            src_ref=zsend.at[h, to], dst_ref=zrecv.at[h, d - 1],
             send_sem=zsend_sem.at[h, d - 1], recv_sem=zrecv_sem.at[h, d - 1],
             device_id=at(y, to, core), device_id_type=MESH)
 
-    for h in range(2):
+    def send_z(h):
         core_copy(3, h).wait_recv()
-        for cp in y_copies(h)[2:]:
-            cp.wait_recv()
-
-        for base in (0, 8):
-            for m, v in enumerate(summed(3, h, base), base):
-                v = v + yleft[h, m].astype(F32) + yright[h, m].astype(F32)
-                own[h, m] = v
-                zsend[h, m] = v.astype(BF16)
+        for k in range(2, 6):
+            y_copy(h, k).wait_recv()
+        for m, v in enumerate(summed(3, h, 0, 8)):
+            v = v + yleft[h, m].astype(F32) + yright[h, m].astype(F32)
+            own[h, m] = v
+            zsend[h, m] = v.astype(BF16)
         for d in (4, 3, 5, 2, 6, 1, 7):
             z_copy(h, d).start()
-    for h in range(2):
+
+    here = lanes_at(me, 32)
+
+    def x_copy(h):
+        return pltpu.make_async_remote_copy(
+            src_ref=xsend.at[h], dst_ref=out.at[here], send_sem=xsend_sem.at[h], recv_sem=xrecv_sem.at[h],
+            device_id=(aux, owner[h]), device_id_type=MESH)
+
+    def finish(h):
         for d in range(1, 8):
             z_copy(h, d).wait_recv()
-        for m in range(2):
-            v = own[h, z * 2 + m]
-            for d in range(7):
-                v = v + zrecv[h, d, m].astype(F32)
-            xsend[2 * h + m] = v
-
-    here = lanes_at(me, 32)
-    out[here, :] = xsend[me]
-
-    def x_copy(d):
-        to = lax.rem(me + d, 4)
-        return pltpu.make_async_remote_copy(
-            src_ref=xsend.at[to], dst_ref=out.at[here],
-            send_sem=xsend_sem.at[d - 1], recv_sem=xrecv_sem.at[d - 1],
-            device_id=(aux, to), device_id_type=MESH)
-
-    for d in (2, 1, 3):
-        x_copy(d).start()
+        v = own[h, z]
+        for d in range(7):
+            v = v + zrecv[h, d].astype(F32)
+        if h < 3:
+            xsend[h] = v
+            x_copy(h).start()
+        else:
+            out[here, :] = v
+
+    def shares(*parts):
+        for n, h in parts:
+            share(n, h)
+
+    shares((0, 0), (1, 0), (2, 0), (0, 1))
+    send_direct(0)
+    shares((1, 1), (2, 1), (0, 2))
+    send_direct(1)
+    send_merged(0)
+    shares((1, 2), (2, 2), (0, 3))
+    send_direct(2)
+    send_merged(1)
+    shares((1, 3), (2, 3), (3, 0), (3, 1))
+    send_direct(3)
+    send_z(0)
+    send_merged(2)
+    shares((3, 2), (3, 3))
+    send_z(1)
+    send_merged(3)
+    finish(0)
+    send_z(2)
+    finish(1)
+    send_z(3)
+    finish(2)
+    finish(3)
+
     for c in range(NCHUNK):
         to_left(c).wait_send()
         to_right(c).wait_send()
         onward(c).wait_send()
-    for h in range(2):
+    for h in range(4):
         for n in range(4):
             core_copy(n, h).wait_send()
-        for cp in y_copies(h):
-            cp.wait_send()
+        for k in range(6):
+            y_copy(h, k).wait_send()
         for d in range(1, 8):
             z_copy(h, d).wait_send()
-    for d in range(1, 4):
-        x_copy(d).wait()
+        if h < 3:
+            x_copy(h).wait()
 
 
 def applied(cols, rows, live, row_lanes, integrals, orbitals):
@@ -328,20 +329,20 @@
             vmem((NCHUNK, 512, CT), BF16),
             vmem((64, 512), F32),
             vmem((SLOTS + 1, 32, 128), F32),
-            vmem((2, 16, 32, 128), F32),
-            vmem((8, 16, 32, 128), BF16),
-            vmem((8, 16, 32, 128), BF16),
-            vmem((2, 6, 8, 32, 128), BF16),
-            vmem((2, 2, 8, 32, 128), BF16),
-            vmem((2, 16, 32, 128), BF16),
-            vmem((2, 16, 32, 128), BF16),
-            vmem((2, 16, 32, 128), BF16),
-            vmem((2, 7, 2, 32, 128), BF16),
-            vmem((4, 32, 128), F32),
+            vmem((4, 8, 32, 128), F32),
+            vmem((16, 8, 32, 128), BF16),
+            vmem((16, 8, 32, 128), BF16),
+            vmem((4, 6, 4, 32, 128), BF16),
+            vmem((4, 2, 4, 32, 128), BF16),
+            vmem((4, 8, 32, 128), BF16),
+            vmem((4, 8, 32, 128), BF16),
+            vmem((4, 8, 32, 128), BF16),
+            vmem((4, 7, 32, 128), BF16),
+            vmem((3, 32, 128), F32),
             sem, sem, sem((NCHUNK,)),
             sem((NCHUNK,)), sem((NCHUNK,)), sem((NCHUNK,)),
             sem((NCHUNK,)), sem((NCHUNK,)), sem((NCHUNK,)),
-            sem((8,)), sem((8,)), sem((2, 6)), sem((2, 6)), sem((2, 7)), sem((2, 7)), sem((3,)), sem((3,)),
+            sem((16,)), sem((16,)), sem((4, 6)), sem((4, 6)), sem((4, 7)), sem((4, 7)), sem((3,)), sem((3,)),
         ],
         compiler_params=pltpu.CompilerParams(
             collective_id=0, has_side_effects=True, vmem_limit_bytes=58 * 1024 * 1024),

time: 60.5 us -> 57.7 us (0.954); the launches traced: 59.7 us -> 57.5 us
  Pallas kernels: 57.5 us -> 55.4 us
    pallas_call x1, Pallas kernels: 57.5 us -> 55.4 us  [applied(): pl.pallas_call(kernel, out_shape=jax.ShapeDtypeStruct((128, 128), F32), i...]
where the time goes in v5:
time: 57.7 us; the launch traced here: 57.5 us
  Pallas kernels  55.4 us (96%)
  local copies, waits for them, and re-layouts  1.47 us (3%)
  between operations  0.66 us (1%)
    pallas_call x1, Pallas kernels, applied(): pl.pallas_call(kernel, out_shape=jax.ShapeDtypeStruct((128, 128), F32), i...  55.4 us
    unnamed x1, local copies, waits for them, and re-layouts  1.47 us

profile of v5, /device:TPU:6, one launch (start us, length us, event | category | flops | bytes accessed | tf_op | source)
XLA Modules:
  0.0 57.5 jit_solution(12285891501804423875)
XLA Ops:
  0.7 55.4 %shard_map.55 = f32[128,128]{1,0:T(8,128)} custom-call(s32[128]{0:T(128)} %cols.1, s32[128]{0:T(128)} %rows.1, s32[1]{0:T(128)S(6)} %copy.7.live, s32[1,128]{1,0:T(1,128)} %bitcast.3, bf16[8192,512]{1,0:T(8,128)(2,1)} %bitcast.2, bf16[32,32768]{1,0:T(8,128)(2,1)} %orbitals.1), custom_call_target="tpu_custom_call" | custom-call | tf_op jit(solution)/shard_map/pallas_call | solution.py:315
  56.1 1.5 %copy.8 = f32[128,128]{1,0:T(8,128)} copy(f32[128,128]{1,0:T(8,128)} %shard_map.55) | data formatting | bytes 131072

commit v6 on v5

--- a/solution.py
+++ b/solution.py
@@ -216,10 +216,12 @@
             ysend[h, k, m] = v.astype(BF16)
         y_copy(h, k).start()
 
-    def send_direct(h):
+    def send_far(h):
         core_copy(0, h).wait_recv()
         fill(h, 0, summed(0, h, 0, 4))
         fill(h, 1, summed(0, h, 4, 4))
+
+    def send_near(h):
         core_copy(1, h).wait_recv()
         fill(h, 2, summed(1, h, 4, 4))
         core_copy(2, h).wait_recv()
@@ -272,21 +274,25 @@
         for n, h in parts:
             share(n, h)
 
-    shares((0, 0), (1, 0), (2, 0), (0, 1))
-    send_direct(0)
-    shares((1, 1), (2, 1), (0, 2))
-    send_direct(1)
+    shares((0, 0), (1, 0), (2, 0), (0, 1), (0, 2))
+    send_far(0)
+    send_near(0)
+    send_far(1)
+    send_far(2)
+    shares((0, 3), (1, 1), (2, 1))
     send_merged(0)
-    shares((1, 2), (2, 2), (0, 3))
-    send_direct(2)
+    send_far(3)
+    shares((3, 0), (1, 2), (2, 2))
+    send_near(1)
     send_merged(1)
-    shares((1, 3), (2, 3), (3, 0), (3, 1))
-    send_direct(3)
+    shares((3, 1), (1, 3), (2, 3))
+    send_near(2)
     send_z(0)
     send_merged(2)
     shares((3, 2), (3, 3))
+    send_near(3)
+    send_merged(3)
     send_z(1)
-    send_merged(3)
     finish(0)
     send_z(2)
     finish(1)

time: 57.7 us -> 57.6 us (level)
  no operation moved by 1% of the time
where the time goes in v6:
time: 57.6 us; the launch traced here: 57.4 us
  Pallas kernels  55.3 us (96%)
  local copies, waits for them, and re-layouts  1.47 us (3%)
  between operations  0.66 us (1%)
    pallas_call x1, Pallas kernels, applied(): pl.pallas_call(kernel, out_shape=jax.ShapeDtypeStruct((128, 128), F32), i...  55.3 us
    unnamed x1, local copies, waits for them, and re-layouts  1.47 us

profile of v6, /device:TPU:6, one launch (start us, length us, event | category | flops | bytes accessed | tf_op | source)
XLA Modules:
  0.0 57.4 jit_solution(16175381515579430050)
XLA Ops:
  0.7 55.3 %shard_map.55 = f32[128,128]{1,0:T(8,128)} custom-call(s32[128]{0:T(128)} %cols.1, s32[128]{0:T(128)} %rows.1, s32[1]{0:T(128)S(6)} %copy.7.live, s32[1,128]{1,0:T(1,128)} %bitcast.3, bf16[8192,512]{1,0:T(8,128)(2,1)} %bitcast.2, bf16[32,32768]{1,0:T(8,128)(2,1)} %orbitals.1), custom_call_target="tpu_custom_call" | custom-call | tf_op jit(solution)/shard_map/pallas_call | solution.py:321
  56.0 1.5 %copy.8 = f32[128,128]{1,0:T(8,128)} copy(f32[128,128]{1,0:T(8,128)} %shard_map.55) | data formatting | bytes 131072
